TPU v7x, 32 devices: a whole 2x2x4 slice. The times are simulated.
32 devices in a mesh: row: 4 (over y, core), col: 8 (over z, x).
Axes of the slice: x: 2, y: 2, z: 4, core: 2. Of those that a mesh axis runs over, the one named last changes fastest.
Arguments:
- wavefield: bfloat16 [32768, 2, 128], P(('col', 'row')), may hold values from -6 to 6
- recorded: bfloat16 [32768, 2, 128], P(('row', 'col')), may hold values from -6 to 6
- v_bases: bfloat16 [128, 128, 32, 256], P('row', 'col'), may hold values from -0.25 to 0.25
- u_bases: bfloat16 [128, 128, 32, 256], P(('row', 'col')), may hold values from -0.09375 to 0.09375
- ranks: int32 [128, 128], P('row', 'col'), may hold values from 1 to 16
Outputs:
- residual: float32 [32768, 2, 128], P(('row', 'col'))
- gradient: float32 [32768, 2, 128], P(('col', 'row'))
Inputs may be any that keep to these rules, and one draw needn't show every extreme that they name: `ranks`: some tile has rank 16.
All inputs are finite; a program needn't handle non-finite values.
Results may differ from a plain program's by a relative error of at most 0.0038.
Values may be sent and summed in bfloat16 or wider, within the bound.
A program may use at most 128 MiB of HBM per device.

v0:
```python
import jax
import jax.numpy as jnp
from jax import lax
from jax.sharding import PartitionSpec as P


def combine_adjoint(prod):
    half = prod.shape[2] // 2
    real = prod[:, :, :half, 0] + prod[:, :, half:, 1]
    imag = prod[:, :, :half, 1] - prod[:, :, half:, 0]
    return jnp.stack([real, imag], axis=3)


def stacked(coeffs):
    real = coeffs[:, :, :, 0]
    imag = coeffs[:, :, :, 1]
    first = jnp.concatenate([real, -imag], axis=2)
    second = jnp.concatenate([imag, real], axis=2)
    return jnp.stack([first, second], axis=3)


def v_adjoint(bases, blocks, mask):
    prod = jnp.einsum("ijrk,jkcs->ijrcs", bases, blocks, preferred_element_type=jnp.float32)
    return (combine_adjoint(prod) * mask[:, :, :, None, None]).astype(jnp.bfloat16)


def u_apply(bases, coeffs):
    return jnp.einsum(
        "ijrk,ijrcs->ikcs", bases, stacked(coeffs), preferred_element_type=jnp.float32
    )


def u_adjoint(bases, rows):
    prod = jnp.einsum("ijrk,ikcs->ijrcs", bases, rows, preferred_element_type=jnp.float32)
    return combine_adjoint(prod).astype(jnp.bfloat16)


def v_apply(bases, back, mask):
    masked = back * mask.astype(jnp.bfloat16)[:, :, :, None, None]
    return jnp.einsum(
        "ijrk,ijrcs->jkcs", bases, stacked(masked), preferred_element_type=jnp.float32
    )


def body(wavefield, recorded, v_bases, u_bases, ranks):
    tile = v_bases.shape[3]
    rank = v_bases.shape[2] // 2
    sources = wavefield.shape[2]
    levels = lax.broadcasted_iota(jnp.int32, (ranks.shape[0], ranks.shape[1], rank), 2)
    mask = (levels < ranks[:, :, None]).astype(jnp.float32)
    gathered = lax.all_gather(wavefield, "row", axis=0, tiled=True)
    blocks = gathered.reshape(-1, tile, 2, sources)
    coeffs = v_adjoint(v_bases, blocks, mask)
    modelled = u_apply(
        u_bases, lax.all_to_all(coeffs, "col", split_axis=0, concat_axis=1, tiled=True)
    )
    residual = modelled.reshape(-1, 2, sources) - recorded.astype(jnp.float32)
    rounded = residual.astype(jnp.bfloat16)
    back = u_adjoint(u_bases, rounded.reshape(-1, tile, 2, sources))
    column_terms = v_apply(
        v_bases, lax.all_to_all(back, "col", split_axis=1, concat_axis=0, tiled=True), mask
    )
    gradient = lax.psum_scatter(
        column_terms.reshape(-1, 2, sources), "row", scatter_dimension=0, tiled=True
    )
    return (residual, gradient)


def solution(mesh):
    in_specs = (
        P(("col", "row"), None, None),
        P(("row", "col"), None, None),
        P("row", "col", None, None),
        P(("row", "col"), None, None, None),
        P("row", "col"),
    )
    out_specs = (P(("row", "col"), None, None), P(("col", "row"), None, None))
    return jax.shard_map(body, mesh=mesh, in_specs=in_specs, out_specs=out_specs, check_vma=False)
```

profile of v0, /device:TPU:27, one launch (start us, length us, event | category | flops | bytes accessed | tf_op | source)
XLA Modules:
  0.0 406.6 jit_solution(10876301127629964826)
XLA Ops:
  7.2 0.0 all-gather.2.cloned.1.call-start
  7.2 1.9 copy.55
  9.1 0.0 all-gather.2.cloned.1.call-update
  9.1 0.0 reduce-scatter.2.cloned.1.call-start
  9.2 0.8 fusion.28
  10.0 24.1 %all-gather.2.cloned.1.call-done = bf16[4096,2,128]{2,0,1:T(8,128)(2,1)} async-done(((bf16[1024,2,128]{2,0,1:T(8,128)(2,1)}), bf16[4096,2,128]{2,0,1:T(8,128)(2,1)}) %all-gather.2.cloned.1.call-update) | async-done | bytes 2097168 | tf_op jit(solution)/shard_map/all_gather | solution.py:51
  34.1 12.1 %convolution_bitcast_fusion.1 = f32[32,16,32,2,128]{4,2,0,3,1:T(8,128)} fusion(bf16[16,256,2,128,1]{3,1,0,2,4:T(8,128)(2,1)} %bitcast.73, bf16[32,16,32,256]{3,2,1,0:T(8,128)(2,1)} %param.7), kind=kOutput, calls=%fused_computation.1 | convolution fusion | flops 2147483648 | bytes 27262976 | tf_op jit(solution)/shard_map/ijrk,jkcs->ijrcs/dot_general | solution.py:23
  46.2 9.2 %slice_add_fusion.1 = (f32[32,16,16,1,128]{4,2,0,3,1:T(8,128)S(1)}, f32[32,16,16,1,128]{4,2,0,3,1:T(8,128)}) fusion(f32[32,16,32,2,128]{4,2,0,3,1:T(8,128)} %convolution_bitcast_fusion.1), kind=kLoop, calls=%fused_computation.21 | loop fusion | flops 2097152 | bytes 25165824 | tf_op jit(solution)/shard_map/add | solution.py:9
  55.5 3.8 fusion
  59.2 1.2 copy.58
  60.4 96.5 %all_to_all.36 = bf16[32,16,16,2,128]{4,2,3,1,0:T(8,128)(2,1)S(1)} all-to-all(bf16[32,16,16,2,128]{4,2,3,1,0:T(8,128)(2,1)S(1)} %copy.58), channel_id=1, replica_groups=mesh['row'=4,'col'=8] {'col'}, dimensions={0} | all-to-all | bytes 8388608 | tf_op jit(solution)/shard_map/all_to_all | solution.py:55
  157.0 1.2 copy.59
  158.1 2.7 fusion.33
  160.9 3.4 copy.98
  164.3 1.6 bitcast_negate_fusion
  165.9 4.5 %copy.97 = bf16[4,128,16,1,128]{1,4,2,0,3:T(8,128)(2,1)} copy(bf16[4,128,16,1,128]{4,2,3,1,0:T(8,128)(2,1)} %get-tuple-element.17) | data formatting | bytes 4194304
  170.4 3.5 maximum_bitcast_fusion
  173.9 0.0 copy-start
  173.9 14.9 %fusion.21 = f32[4,256,2,128]{1,3,2,0:T(8,128)S(1)} fusion(bf16[4,128,32,256,1]{3,2,1,0,4:T(8,128)(2,1)} %bitcast.69, bf16[4,128,32,1,128]{1,4,2,3,0:T(8,128)(2,1)S(1)} %get-tuple-element.21, bf16[4,128,32,1,128]{1,4,2,3,0:T(8,128)(2,1)S(1)} %get-tuple-element.20), kind=kOutput, calls=%fused_computation.32 | convolution fusion | flops 2151677952 | bytes 17825792 | tf_op jit(solution)/shard_map/ijrk,ijrcs->ikcs/dot_general | solution.py:28
  188.7 0.3 copy.64
  189.1 0.0 copy-done
  189.1 0.1 fusion.32
  189.2 25.1 %convolution_bitcast_fusion = f32[4,128,32,2,128]{1,4,2,3,0:T(8,128)} fusion(bf16[4,128,32,256,1]{3,2,1,0,4:T(8,128)(2,1)} %bitcast.70, bf16[4,256,2,128,1]{3,1,0,2,4:T(8,128)(2,1)S(1)} %bitcast.72), kind=kOutput, calls=%fused_computation | convolution fusion | flops 2147483648 | bytes 25690112 | tf_op jit(solution)/shard_map/ijrk,ikcs->ijrcs/dot_general | solution.py:34
  214.3 6.8 %fusion.14 = (bf16[4,128,16,1,128]{1,4,2,3,0:T(8,128)(2,1)S(1)}, bf16[4,128,16,1,128]{1,4,2,3,0:T(8,128)(2,1)S(1)}) fusion(f32[4,128,32,2,128]{1,4,2,3,0:T(8,128)} %convolution_bitcast_fusion), kind=kLoop, calls=%fused_computation.19 | loop fusion | flops 4194304 | bytes 20971520 | tf_op jit(solution)/shard_map/convert
  221.1 2.3 pad_maximum_fusion
  223.4 7.9 %copy.68 = bf16[4,128,16,2,128]{4,2,3,0,1:T(8,128)(2,1)} copy(bf16[4,128,16,2,128]{1,4,2,3,0:T(8,128)(2,1)} %pad_maximum_fusion) | data formatting | bytes 8388608 | tf_op jit(solution)/shard_map/stack | solution.py:11
  231.3 96.4 %all_to_all.37 = bf16[4,128,16,2,128]{4,2,3,0,1:T(8,128)(2,1)S(1)} all-to-all(bf16[4,128,16,2,128]{4,2,3,0,1:T(8,128)(2,1)} %copy.68), channel_id=1, replica_groups=mesh['row'=4,'col'=8] {'col'}, dimensions={1} | all-to-all | bytes 8388608 | tf_op jit(solution)/shard_map/all_to_all | solution.py:61
  327.8 1.3 copy.70
  329.0 1.2 broadcast_multiply_fusion
  330.3 1.1 slice_bitcast_fusion
  331.4 0.3 fusion.31
  331.7 4.1 %maximum_bitcast_fusion.2 = (bf16[32,16,32,1,128]{4,2,0,3,1:T(8,128)(2,1)}, bf16[32,16,32,1,128]{4,2,0,3,1:T(8,128)(2,1)}) fusion(bf16[32,16,16,128]{3,2,0,1:T(8,128)(2,1)S(1)} %fusion.31, bf16[32,16,16,128]{3,2,0,1:T(8,128)(2,1)S(1)} %get-tuple-element.15, bf16[32,16,16,128]{3,2,0,1:T(8,128)(2,1)S(1)} %get-tuple-element.14), kind=kLoop, calls=%fused_computation.25 | loop fusion | flops 16777216 | bytes 14680064 | tf_op jit(solution)/shard_map/stack | solution.py:19
  335.9 10.5 %fusion.15 = f32[16,256,2,128]{1,3,2,0:T(8,128)} fusion(bf16[32,16,32,1,128]{4,2,0,3,1:T(8,128)(2,1)} %get-tuple-element.19, bf16[32,16,32,1,128]{4,2,0,3,1:T(8,128)(2,1)} %get-tuple-element.18, bf16[32,16,32,256]{3,2,1,0:T(8,128)(2,1)} %param.7), kind=kOutput, calls=%fused_computation.27 | convolution fusion | flops 2151677952 | bytes 20971520 | tf_op jit(solution)/shard_map/ijrk,ijrcs->jkcs/dot_general | solution.py:40
  346.3 5.4 %copy.73 = f32[16,256,2,128]{3,1,0,2:T(8,128)} copy(f32[16,256,2,128]{1,3,2,0:T(8,128)} %fusion.15) | data formatting | bytes 8388608 | tf_op jit(solution)/shard_map/ijrk,ijrcs->jkcs/dot_general | solution.py:40
  351.7 0.0 reduce-scatter.2.cloned.1.call-update
  351.7 1.8 copy.74
  353.5 43.2 %reduce-scatter.2.cloned.1.call-done = f32[1024,2,128]{2,0,1:T(8,128)} async-done(((f32[4096,2,128]{2,0,1:T(8,128)}), f32[1024,2,128]{2,0,1:T(8,128)}) %reduce-scatter.2.cloned.1.call-update) | async-done | bytes 1048592 | tf_op jit(solution)/shard_map/reduce_scatter | solution.py:63
  396.7 3.0 copy.75
Async XLA Ops:
  7.2 27.0 %all-gather.2.cloned.1.call-start = ((), (), s32[]{:S(2)}) async-start(), calls=%async_computation.3 | async-start | bytes 2621440 | tf_op jit(solution)/shard_map/all_gather | solution.py:51
  9.1 387.6 %reduce-scatter.2.cloned.1.call-start = ((), (), s32[]{:S(2)}) async-start(), calls=%async_computation.4 | async-start | bytes 5242880 | tf_op jit(solution)/shard_map/reduce_scatter | solution.py:63
  173.9 15.2 %copy-start = (bf16[1024,2,128]{2,1,0:T(2,128)(2,1)S(1)}, bf16[1024,2,128]{2,1,0:T(2,128)(2,1)}, u32[]{:S(2)}) copy-start(bf16[1024,2,128]{2,1,0:T(2,128)(2,1)} %param.6) | copy-start | bytes 1572868
Sparse Core Ops, SparseCore 0:
  10.1 23.9 all-gather.1
  351.8 44.8 reduce-scatter.1
where the time goes:
time: 409 us; the launch traced here: 407 us
  blocking collectives  193 us (47%)
  waiting for transfers between devices  67.3 us (16%)
  matrix products  62.5 us (15%)
  local copies, waits for them, and re-layouts  35.7 us (9%)
  other arithmetic  33.8 us (8%)
  between operations  14.2 us (3%)
    all_to_all x1, blocking collectives, body(): lax.all_to_all(coeffs, 'col', split_axis=0, concat_axis=1, tiled=True)  96.5 us
    all_to_all x1, blocking collectives, body(): lax.all_to_all(back, 'col', split_axis=1, concat_axis=0, tiled=True)  96.4 us
    reduce_scatter x1, waiting for transfers between devices, body(): lax.psum_scatter(column_terms.reshape(-1, 2, sources), 'row', scatter_dim...  43.2 us
    dot_general x1, matrix products, u_adjoint(): jnp.einsum('ijrk,ikcs->ijrcs', bases, rows, preferred_element_type=jnp.fl...  25.1 us
    all_gather x1, waiting for transfers between devices, body(): gathered = lax.all_gather(wavefield, 'row', axis=0, tiled=True)  24.1 us
    dot_general x1, matrix products, u_apply(): jnp.einsum('ijrk,ijrcs->ikcs', bases, stacked(coeffs), preferred_element_...  14.9 us
    unnamed x7, local copies, waits for them, and re-layouts  14.6 us
    dot_general x1, matrix products, v_adjoint(): jnp.einsum('ijrk,jkcs->ijrcs', bases, blocks, preferred_element_type=jnp....  12.1 us
  transfers between devices with their start and end apart: 2, of which 2 were waited for; matrix products, arithmetic and copies ran while one was open for 1% of the time, Pallas kernels for 0%

commit v1 on v0

v1 whole, which is shorter than its diff:
```python
import functools

import jax
import jax.numpy as jnp
from jax import lax
from jax.experimental import pallas as pl
from jax.experimental.pallas import tpu as pltpu
from jax.sharding import PartitionSpec as P

MESH = pl.DeviceIdType.MESH


def adjoint_pair(prod, half):
    sources = prod.shape[-1] // 2
    prod = prod.reshape(-1, 2, half, 2 * sources)
    first, second = prod[:, 0], prod[:, 1]
    real = first[..., :sources] + second[..., sources:]
    imag = first[..., sources:] - second[..., :sources]
    return jnp.concatenate([real, imag], axis=-1)


def stacked(coeffs):
    sources = coeffs.shape[-1] // 2
    real, imag = coeffs[..., :sources], coeffs[..., sources:]
    second = jnp.concatenate([-imag, real], axis=-1)
    both = jnp.concatenate([coeffs, second], axis=1)
    return both.reshape(-1, 2 * sources)


def flat(bases):
    return bases.reshape(-1, bases.shape[-1])


def transposed_dot(left, right):
    return lax.dot_general(left, right, (((0,), (0,)), ((), ())), preferred_element_type=jnp.float32)


def kernel(
    n_row, n_col, wave, rec, v, u, ranks, res, grad,
    x, send1, recv1, send2, recv2, total, rs1, sb, rs2,
    xs, xr, s1, r1, s2, r2, gs1, gr1, gs2, gr2,
):
    row, col = lax.axis_index("row"), lax.axis_index("col")
    y, core = row // 2, row % 2
    n_y = n_row // 2
    tiles, columns = u.shape[0], v.shape[2]
    half = v.shape[3] // 2
    width = wave.shape[0]
    level = lax.broadcasted_iota(jnp.int32, (half, x.shape[2]), 0)

    barrier = pltpu.get_barrier_semaphore()
    for k in range(1, n_col):
        pl.semaphore_signal(barrier, inc=1, device_id={"col": lax.rem(col + k, n_col)}, device_id_type=MESH)
    for k in range(1, n_row):
        pl.semaphore_signal(barrier, inc=1, device_id={"row": lax.rem(row + k, n_row)}, device_id_type=MESH)
    pl.semaphore_wait(barrier, n_col + n_row - 2)

    def wave_copy(peer, origin):
        return pltpu.make_async_remote_copy(
            src_ref=wave, dst_ref=x.at[pl.ds(origin * width, width)],
            send_sem=xs.at[peer], recv_sem=xr.at[origin],
            device_id={"row": peer}, device_id_type=MESH)

    def exchange(src, dst, send_sem, recv_sem, a, peer, origin):
        return pltpu.make_async_remote_copy(
            src_ref=src.at[a, peer], dst_ref=dst.at[a, origin],
            send_sem=send_sem.at[a, peer], recv_sem=recv_sem.at[a, origin],
            device_id={"col": peer}, device_id_type=MESH)

    for k in range(1, n_row):
        wave_copy(lax.rem(row + k, n_row), row).start()
    x[pl.ds(row * width, width)] = wave[...]
    total[...] = jnp.zeros_like(total)
    for a in range(tiles):
        res[a] = -rec[a].astype(jnp.float32)
    for k in range(1, n_row):
        peer = lax.rem(row + k, n_row)
        wave_copy(peer, peer).wait_recv()

    def forward(a, carry):
        def one(j, carry):
            prod = jnp.dot(flat(v[:, a, j]), x[j], preferred_element_type=jnp.float32)
            coeffs = adjoint_pair(prod, half)
            for d in range(n_col):
                kept = jnp.where(level < ranks[d * tiles + a, j], coeffs[d], 0.0)
                send1[a, d, j] = kept.astype(jnp.bfloat16)
            return carry

        lax.fori_loop(0, columns, one, 0)
        for k in range(1, n_col):
            exchange(send1, recv1, s1, r1, a, lax.rem(col + k, n_col), col).start()
        recv1[a, col] = send1[a, col]
        return carry

    lax.fori_loop(0, tiles, forward, 0)

    def middle(a, carry):
        def apply(k, carry):
            origin = lax.rem(col + n_col - k, n_col)

            @pl.when(k > 0)
            def _():
                exchange(send1, recv1, s1, r1, a, origin, origin).wait_recv()

            res[a] += transposed_dot(flat(u[a, origin]), stacked(recv1[a, origin]))
            return carry

        lax.fori_loop(0, n_col, apply, 0)
        rounded = res[a].astype(jnp.bfloat16)

        def project(k, carry):
            peer = lax.rem(col + k, n_col)
            prod = jnp.dot(flat(u[a, peer]), rounded, preferred_element_type=jnp.float32)
            send2[a, peer] = adjoint_pair(prod, half).astype(jnp.bfloat16)

            @pl.when(k < n_col)
            def _():
                exchange(send2, recv2, s2, r2, a, peer, col).start()

            return carry

        lax.fori_loop(1, n_col + 1, project, 0)
        recv2[a, col] = send2[a, col]
        return carry

    lax.fori_loop(0, tiles, middle, 0)

    def last(a, carry):
        for k in range(1, n_col):
            origin = lax.rem(col + n_col - k, n_col)
            exchange(send2, recv2, s2, r2, a, origin, origin).wait_recv()

        def one(j, carry):
            kept = [
                jnp.where(level < ranks[s * tiles + a, j], recv2[a, s, j].astype(jnp.float32), 0.0).astype(jnp.bfloat16)
                for s in range(n_col)
            ]
            total[j] += transposed_dot(flat(v[:, a, j]), stacked(jnp.stack(kept)))
            return carry

        lax.fori_loop(0, columns, one, 0)
        return carry

    lax.fori_loop(0, tiles, last, 0)

    def core_copy(k):
        return pltpu.make_async_remote_copy(
            src_ref=total.at[pl.ds((2 * k + 1 - core) * width, width)], dst_ref=rs1.at[k],
            send_sem=gs1.at[k], recv_sem=gr1.at[k],
            device_id={"row": 2 * y + 1 - core}, device_id_type=MESH)

    def chip_copy(peer, origin):
        return pltpu.make_async_remote_copy(
            src_ref=sb.at[peer], dst_ref=rs2.at[origin],
            send_sem=gs2.at[peer], recv_sem=gr2.at[origin],
            device_id={"row": 2 * peer + core}, device_id_type=MESH)

    order = [lax.rem(y + k, n_y) for k in range(1, n_y)]
    for peer in order + [y]:
        core_copy(peer).start()
    for peer in order:
        core_copy(peer).wait_recv()
        here = total[pl.ds((2 * peer + core) * width, width)]
        sb[peer] = (here + rs1[peer]).astype(jnp.bfloat16)
        chip_copy(peer, y).start()
    core_copy(y).wait_recv()
    grad[...] = total[pl.ds(row * width, width)] + rs1[y]
    for peer in order:
        chip_copy(peer, peer).wait_recv()
        grad[...] += rs2[peer].astype(jnp.float32)

    for k in range(1, n_row):
        wave_copy(lax.rem(row + k, n_row), row).wait_send()
    for k in range(n_y):
        core_copy(k).wait_send()
    for peer in order:
        chip_copy(peer, y).wait_send()

    def drain(a, carry):
        for k in range(1, n_col):
            peer = lax.rem(col + k, n_col)
            exchange(send1, recv1, s1, r1, a, peer, col).wait_send()
            exchange(send2, recv2, s2, r2, a, peer, col).wait_send()
        return carry

    lax.fori_loop(0, tiles, drain, 0)


def body(n_row, n_col, wavefield, recorded, v_bases, u_bases, ranks):
    tile, sources = v_bases.shape[3], wavefield.shape[2]
    both, half = v_bases.shape[2], v_bases.shape[2] // 2
    tiles, columns = u_bases.shape[0], v_bases.shape[1]
    wide = 2 * sources
    width = columns // n_row
    vmem = pl.BlockSpec(memory_space=pltpu.VMEM)
    trade = pltpu.VMEM((tiles, n_col, columns, half, wide), jnp.bfloat16)
    dma = pltpu.SemaphoreType.DMA
    residual, gradient = pl.pallas_call(
        functools.partial(kernel, n_row, n_col),
        out_shape=(
            jax.ShapeDtypeStruct((tiles, tile, wide), jnp.float32),
            jax.ShapeDtypeStruct((width, tile, wide), jnp.float32),
        ),
        in_specs=[vmem, vmem, vmem, vmem, pl.BlockSpec(memory_space=pltpu.SMEM)],
        out_specs=(vmem, vmem),
        scratch_shapes=[
            pltpu.VMEM((columns, tile, wide), jnp.bfloat16),
            trade, trade, trade, trade,
            pltpu.VMEM((columns, tile, wide), jnp.float32),
            pltpu.VMEM((n_row // 2, width, tile, wide), jnp.float32),
            pltpu.VMEM((n_row // 2, width, tile, wide), jnp.bfloat16),
            pltpu.VMEM((n_row // 2, width, tile, wide), jnp.bfloat16),
            dma((n_row,)), dma((n_row,)),
            dma((tiles, n_col)), dma((tiles, n_col)), dma((tiles, n_col)), dma((tiles, n_col)),
            dma((n_row // 2,)), dma((n_row // 2,)), dma((n_row // 2,)), dma((n_row // 2,)),
        ],
        compiler_params=pltpu.CompilerParams(
            collective_id=0, has_side_effects=True, vmem_limit_bytes=58 * 2**20
        ),
    )(
        wavefield.reshape(width, tile, wide),
        recorded.reshape(tiles, tile, wide),
        v_bases.reshape(n_col, tiles, columns, both, tile),
        u_bases.reshape(tiles, n_col, columns, both, tile),
        ranks,
    )
    return residual.reshape(-1, 2, sources), gradient.reshape(-1, 2, sources)


def solution(mesh):
    in_specs = (
        P(("col", "row"), None, None),
        P(("row", "col"), None, None),
        P("row", "col", None, None),
        P(("row", "col"), None, None, None),
        P("row", "col"),
    )
    out_specs = (P(("row", "col"), None, None), P(("col", "row"), None, None))
    part = functools.partial(body, mesh.shape["row"], mesh.shape["col"])
    return jax.shard_map(part, mesh=mesh, in_specs=in_specs, out_specs=out_specs, check_vma=False)
```

time: 409 us -> 240 us (0.59)
  Pallas kernels: 0 us -> 225 us
  blocking collectives: 193 us -> 0 us
  waiting for transfers between devices: 67.3 us -> 0 us
  matrix products: 62.5 us -> 0 us
  other arithmetic: 33.8 us -> 0 us
  local copies, waits for them, and re-layouts: 35.7 us -> 11.1 us
  between operations: 14.2 us -> 0.64 us
    pallas_call x0 -> x1, Pallas kernels: none -> 225 us  [body(): pl.pallas_call(functools.partial(kernel, n_row, n_col), out_shape=(jax.Sh...]
    all_to_all x2 -> x0, blocking collectives: 193 us -> none  [the longest x1 96.5 us: body(): lax.all_to_all(coeffs, 'col', split_axis=0, concat_axis=1, tiled=True)]
    dot_general x4 -> x0, matrix products: 62.5 us -> none  [the longest x1 25.1 us: u_adjoint(): jnp.einsum('ijrk,ikcs->ijrcs', bases, rows, preferred_element_type=jnp.fl...]
    reduce_scatter x1 -> x0, waiting for transfers between devices: 43.2 us -> none  [body(): lax.psum_scatter(column_terms.reshape(-1, 2, sources), 'row', scatter_dim...]
    all_gather x1 -> x0, waiting for transfers between devices: 24.1 us -> none  [body(): gathered = lax.all_gather(wavefield, 'row', axis=0, tiled=True)]
    another operation x4 -> x0, other arithmetic: 16.7 us -> none  [the longest x2 7.6 us: stacked(): return jnp.stack([first, second], axis=3)]
    unnamed x7 -> x1, local copies, waits for them, and re-layouts: 14.6 us -> 1.37 us
    reshape x0 -> x4, local copies, waits for them, and re-layouts: none -> 9.75 us  [the longest x2 5.42 us: body(): return (residual.reshape(-1, 2, sources), gradient.reshape(-1, 2, sources))]
  transfers between devices with their start and end apart: 2 -> 0, of which waited for: 2 -> 0; matrix products, arithmetic and copies ran while one was open for 1% -> 0% of each run, Pallas kernels for 0% -> 0%
where the time goes in v1:
time: 240 us; the launch traced here: 237 us
  Pallas kernels  225 us (94%)
  local copies, waits for them, and re-layouts  11.1 us (5%)
    pallas_call x1, Pallas kernels, body(): pl.pallas_call(functools.partial(kernel, n_row, n_col), out_shape=(jax.Sh...  225 us
    reshape x2, local copies, waits for them, and re-layouts, body(): return (residual.reshape(-1, 2, sources), gradient.reshape(-1, 2, sources))  5.42 us

profile of v1, /device:TPU:27, one launch (start us, length us, event | category | flops | bytes accessed | tf_op | source)
XLA Modules:
  0.0 237.0 jit_solution(11122727646560804992)
XLA Ops:
  0.6 1.4 copy.7.ranks
  2.0 2.2 reshape.22.wave
  4.2 2.2 reshape.23.rec
  6.3 225.2 %shard_map.68 = (f32[4,256,256]{2,1,0:T(8,128)}, f32[4,256,256]{2,1,0:T(8,128)}) custom-call(bf16[4,256,256]{2,1,0:T(8,128)(2,1)} %reshape.22.wave, bf16[4,256,256]{2,1,0:T(8,128)(2,1)} %reshape.23.rec, bf16[8,4,16,32,256]{4,3,2,1,0:T(8,128)(2,1)} %bitcast.2, bf16[4,8,16,32,256]{4,3,2,1,0:T(8,128)(2,1)} %bitcast.3, s32[32,16]{1,0:T(8,128)} %copy.7.ranks), custom_call_target="tpu_custom_call" | custom-call | tf_op jit(solution)/shard_map/pallas_call | solution.py:198
  231.6 2.7 %reshape.26 = f32[1024,2,128]{2,1,0:T(2,128)} reshape(f32[4,256,256]{2,1,0:T(8,128)} %get-tuple-element.4) | data formatting | bytes 2097152 | tf_op jit(solution)/shard_map/reshape | solution.py:227
  234.3 2.7 %reshape.27 = f32[1024,2,128]{2,1,0:T(2,128)} reshape(f32[4,256,256]{2,1,0:T(8,128)} %get-tuple-element.5) | data formatting | bytes 2097152 | tf_op jit(solution)/shard_map/reshape | solution.py:227

commit v2 on v1

--- a/solution.py
+++ b/solution.py
@@ -36,9 +36,9 @@
 
 
 def kernel(
-    n_row, n_col, wave, rec, v, u, ranks, res, grad,
-    x, send1, recv1, send2, recv2, total, rs1, sb, rs2,
-    xs, xr, s1, r1, s2, r2, gs1, gr1, gs2, gr2,
+    n_row, n_col, wave, rec, v_hbm, u_hbm, ranks, res, grad,
+    v, u, x, send1, recv1, send2, recv2, total, rs1, sb, rs2,
+    vs, us, xs, xr, s1, r1, s2, r2, gs1, gr1, gs2, gr2,
 ):
     row, col = lax.axis_index("row"), lax.axis_index("col")
     y, core = row // 2, row % 2
@@ -46,7 +46,17 @@
     tiles, columns = u.shape[0], v.shape[2]
     half = v.shape[3] // 2
     width = wave.shape[0]
+    group = 2 * width
     level = lax.broadcasted_iota(jnp.int32, (half, x.shape[2]), 0)
+
+    def v_copy(part):
+        span = pl.ds(part * group, group)
+        return pltpu.make_async_copy(v_hbm.at[:, :, span], v.at[:, :, span], vs.at[part])
+
+    u_copy = pltpu.make_async_copy(u_hbm, u, us)
+    for k in range(n_y):
+        v_copy(lax.rem(y + k, n_y)).start()
+    u_copy.start()
 
     barrier = pltpu.get_barrier_semaphore()
     for k in range(1, n_col):
@@ -61,38 +71,52 @@
             send_sem=xs.at[peer], recv_sem=xr.at[origin],
             device_id={"row": peer}, device_id_type=MESH)
 
-    def exchange(src, dst, send_sem, recv_sem, a, peer, origin):
-        return pltpu.make_async_remote_copy(
-            src_ref=src.at[a, peer], dst_ref=dst.at[a, origin],
-            send_sem=send_sem.at[a, peer], recv_sem=recv_sem.at[a, origin],
+    def exchange(src, dst, send_sem, recv_sem, a, peer, origin, part):
+        span = pl.ds(part * group, group)
+        return pltpu.make_async_remote_copy(
+            src_ref=src.at[a, peer, span], dst_ref=dst.at[a, origin, span],
+            send_sem=send_sem.at[a, peer, part], recv_sem=recv_sem.at[a, origin, part],
             device_id={"col": peer}, device_id_type=MESH)
 
-    for k in range(1, n_row):
-        wave_copy(lax.rem(row + k, n_row), row).start()
+    wave_copy(2 * y + 1 - core, row).start()
+    for k in range(1, n_y):
+        for c in range(2):
+            wave_copy(2 * lax.rem(y + k, n_y) + c, row).start()
     x[pl.ds(row * width, width)] = wave[...]
     total[...] = jnp.zeros_like(total)
     for a in range(tiles):
         res[a] = -rec[a].astype(jnp.float32)
-    for k in range(1, n_row):
-        peer = lax.rem(row + k, n_row)
-        wave_copy(peer, peer).wait_recv()
-
-    def forward(a, carry):
-        def one(j, carry):
-            prod = jnp.dot(flat(v[:, a, j]), x[j], preferred_element_type=jnp.float32)
-            coeffs = adjoint_pair(prod, half)
-            for d in range(n_col):
-                kept = jnp.where(level < ranks[d * tiles + a, j], coeffs[d], 0.0)
-                send1[a, d, j] = kept.astype(jnp.bfloat16)
-            return carry
-
-        lax.fori_loop(0, columns, one, 0)
-        for k in range(1, n_col):
-            exchange(send1, recv1, s1, r1, a, lax.rem(col + k, n_col), col).start()
-        recv1[a, col] = send1[a, col]
-        return carry
-
-    lax.fori_loop(0, tiles, forward, 0)
+
+    for step in range(n_y):
+        part = lax.rem(y + step, n_y)
+        if step == 0:
+            sibling = 2 * y + 1 - core
+            wave_copy(sibling, sibling).wait_recv()
+        else:
+            for c in range(2):
+                wave_copy(2 * part + c, 2 * part + c).wait_recv()
+        v_copy(part).wait()
+
+        def forward(a, carry):
+            def one(t, carry):
+                j = part * group + t
+                prod = jnp.dot(flat(v[:, a, j]), x[j], preferred_element_type=jnp.float32)
+                coeffs = adjoint_pair(prod, half)
+                for d in range(n_col):
+                    kept = jnp.where(level < ranks[d * tiles + a, j], coeffs[d], 0.0)
+                    send1[a, d, j] = kept.astype(jnp.bfloat16)
+                return carry
+
+            lax.fori_loop(0, group, one, 0)
+            for k in range(1, n_col):
+                exchange(send1, recv1, s1, r1, a, lax.rem(col + k, n_col), col, part).start()
+            span = pl.ds(part * group, group)
+            recv1[a, col, span] = send1[a, col, span]
+            return carry
+
+        lax.fori_loop(0, tiles, forward, 0)
+
+    u_copy.wait()
 
     def middle(a, carry):
         def apply(k, carry):
@@ -100,7 +124,8 @@
 
             @pl.when(k > 0)
             def _():
-                exchange(send1, recv1, s1, r1, a, origin, origin).wait_recv()
+                for part in range(n_y):
+                    exchange(send1, recv1, s1, r1, a, origin, origin, part).wait_recv()
 
             res[a] += transposed_dot(flat(u[a, origin]), stacked(recv1[a, origin]))
             return carry
@@ -115,22 +140,26 @@
 
             @pl.when(k < n_col)
             def _():
-                exchange(send2, recv2, s2, r2, a, peer, col).start()
+                for step in range(1, n_y):
+                    exchange(send2, recv2, s2, r2, a, peer, col, lax.rem(y + step, n_y)).start()
 
             return carry
 
         lax.fori_loop(1, n_col + 1, project, 0)
+        for k in range(1, n_col):
+            exchange(send2, recv2, s2, r2, a, lax.rem(col + k, n_col), col, y).start()
         recv2[a, col] = send2[a, col]
         return carry
 
     lax.fori_loop(0, tiles, middle, 0)
 
-    def last(a, carry):
+    def last(a, part):
         for k in range(1, n_col):
             origin = lax.rem(col + n_col - k, n_col)
-            exchange(send2, recv2, s2, r2, a, origin, origin).wait_recv()
-
-        def one(j, carry):
+            exchange(send2, recv2, s2, r2, a, origin, origin, part).wait_recv()
+
+        def one(t, carry):
+            j = part * group + t
             kept = [
                 jnp.where(level < ranks[s * tiles + a, j], recv2[a, s, j].astype(jnp.float32), 0.0).astype(jnp.bfloat16)
                 for s in range(n_col)
@@ -138,10 +167,14 @@
             total[j] += transposed_dot(flat(v[:, a, j]), stacked(jnp.stack(kept)))
             return carry
 
-        lax.fori_loop(0, columns, one, 0)
+        lax.fori_loop(0, group, one, 0)
+
+    def early(a, carry):
+        for step in range(1, n_y + 1):
+            last(a, lax.rem(y + step, n_y))
         return carry
 
-    lax.fori_loop(0, tiles, last, 0)
+    lax.fori_loop(0, tiles - 1, early, 0)
 
     def core_copy(k):
         return pltpu.make_async_remote_copy(
@@ -156,13 +189,16 @@
             device_id={"row": 2 * peer + core}, device_id_type=MESH)
 
     order = [lax.rem(y + k, n_y) for k in range(1, n_y)]
-    for peer in order + [y]:
+    for peer in order:
+        last(tiles - 1, peer)
         core_copy(peer).start()
     for peer in order:
         core_copy(peer).wait_recv()
         here = total[pl.ds((2 * peer + core) * width, width)]
         sb[peer] = (here + rs1[peer]).astype(jnp.bfloat16)
         chip_copy(peer, y).start()
+    last(tiles - 1, y)
+    core_copy(y).start()
     core_copy(y).wait_recv()
     grad[...] = total[pl.ds(row * width, width)] + rs1[y]
     for peer in order:
@@ -179,8 +215,9 @@
     def drain(a, carry):
         for k in range(1, n_col):
             peer = lax.rem(col + k, n_col)
-            exchange(send1, recv1, s1, r1, a, peer, col).wait_send()
-            exchange(send2, recv2, s2, r2, a, peer, col).wait_send()
+            for part in range(n_y):
+                exchange(send1, recv1, s1, r1, a, peer, col, part).wait_send()
+                exchange(send2, recv2, s2, r2, a, peer, col, part).wait_send()
         return carry
 
     lax.fori_loop(0, tiles, drain, 0)
@@ -193,25 +230,30 @@
     wide = 2 * sources
     width = columns // n_row
     vmem = pl.BlockSpec(memory_space=pltpu.VMEM)
+    whole = pl.BlockSpec(memory_space=pl.ANY)
+    n_y = n_row // 2
     trade = pltpu.VMEM((tiles, n_col, columns, half, wide), jnp.bfloat16)
     dma = pltpu.SemaphoreType.DMA
+    pair = dma((tiles, n_col, n_y))
     residual, gradient = pl.pallas_call(
         functools.partial(kernel, n_row, n_col),
         out_shape=(
             jax.ShapeDtypeStruct((tiles, tile, wide), jnp.float32),
             jax.ShapeDtypeStruct((width, tile, wide), jnp.float32),
         ),
-        in_specs=[vmem, vmem, vmem, vmem, pl.BlockSpec(memory_space=pltpu.SMEM)],
+        in_specs=[vmem, vmem, whole, whole, pl.BlockSpec(memory_space=pltpu.SMEM)],
         out_specs=(vmem, vmem),
         scratch_shapes=[
+            pltpu.VMEM((n_col, tiles, columns, both, tile), jnp.bfloat16),
+            pltpu.VMEM((tiles, n_col, columns, both, tile), jnp.bfloat16),
             pltpu.VMEM((columns, tile, wide), jnp.bfloat16),
             trade, trade, trade, trade,
             pltpu.VMEM((columns, tile, wide), jnp.float32),
             pltpu.VMEM((n_row // 2, width, tile, wide), jnp.float32),
             pltpu.VMEM((n_row // 2, width, tile, wide), jnp.bfloat16),
             pltpu.VMEM((n_row // 2, width, tile, wide), jnp.bfloat16),
-            dma((n_row,)), dma((n_row,)),
-            dma((tiles, n_col)), dma((tiles, n_col)), dma((tiles, n_col)), dma((tiles, n_col)),
+            dma((n_y,)), dma, dma((n_row,)), dma((n_row,)),
+            pair, pair, pair, pair,
             dma((n_row // 2,)), dma((n_row // 2,)), dma((n_row // 2,)), dma((n_row // 2,)),
         ],
         compiler_params=pltpu.CompilerParams(

time: 240 us -> 218 us (0.908); the launches traced: 237 us -> 217 us
  Pallas kernels: 225 us -> 206 us
    pallas_call x1, Pallas kernels: 225 us -> 206 us  [body(): pl.pallas_call(functools.partial(kernel, n_row, n_col), out_shape=(jax.Sh...]
where the time goes in v2:
time: 218 us; the launch traced here: 217 us
  Pallas kernels  206 us (94%)
  local copies, waits for them, and re-layouts  11.1 us (5%)
    pallas_call x1, Pallas kernels, body(): pl.pallas_call(functools.partial(kernel, n_row, n_col), out_shape=(jax.Sh...  206 us
    reshape x2, local copies, waits for them, and re-layouts, body(): return (residual.reshape(-1, 2, sources), gradient.reshape(-1, 2, sources))  5.42 us

profile of v2, /device:TPU:27, one launch (start us, length us, event | category | flops | bytes accessed | tf_op | source)
XLA Modules:
  0.0 217.5 jit_solution(220158283311781604)
XLA Ops:
  0.6 1.4 copy.7.ranks
  2.0 2.2 reshape.22.wave
  4.2 2.2 reshape.23.rec
  6.3 205.7 %shard_map.68 = (f32[4,256,256]{2,1,0:T(8,128)}, f32[4,256,256]{2,1,0:T(8,128)}) custom-call(bf16[4,256,256]{2,1,0:T(8,128)(2,1)} %reshape.22.wave, bf16[4,256,256]{2,1,0:T(8,128)(2,1)} %reshape.23.rec, bf16[8,4,16,32,256]{4,3,2,1,0:T(8,128)(2,1)} %bitcast.2, bf16[4,8,16,32,256]{4,3,2,1,0:T(8,128)(2,1)} %bitcast.3, s32[32,16]{1,0:T(8,128)} %copy.7.ranks), custom_call_target="tpu_custom_call" | custom-call | tf_op jit(solution)/shard_map/pallas_call | solution.py:238
  212.1 2.7 %reshape.26 = f32[1024,2,128]{2,1,0:T(2,128)} reshape(f32[4,256,256]{2,1,0:T(8,128)} %get-tuple-element.4) | data formatting | bytes 2097152 | tf_op jit(solution)/shard_map/reshape | solution.py:269
  214.8 2.7 %reshape.27 = f32[1024,2,128]{2,1,0:T(2,128)} reshape(f32[4,256,256]{2,1,0:T(8,128)} %get-tuple-element.5) | data formatting | bytes 2097152 | tf_op jit(solution)/shard_map/reshape | solution.py:269

commit v3 on v2

--- a/solution.py
+++ b/solution.py
@@ -36,8 +36,8 @@
 
 
 def kernel(
-    n_row, n_col, wave, rec, v_hbm, u_hbm, ranks, res, grad,
-    v, u, x, send1, recv1, send2, recv2, total, rs1, sb, rs2,
+    n_row, n_col, wave, rec, v_hbm, u_hbm, ranks, res_out, grad_out,
+    res, v, u, x, send1, recv1, send2, recv2, total, rs1, sb, rs2,
     vs, us, xs, xr, s1, r1, s2, r2, gs1, gr1, gs2, gr2,
 ):
     row, col = lax.axis_index("row"), lax.axis_index("col")
@@ -84,9 +84,6 @@
             wave_copy(2 * lax.rem(y + k, n_y) + c, row).start()
     x[pl.ds(row * width, width)] = wave[...]
     total[...] = jnp.zeros_like(total)
-    for a in range(tiles):
-        res[a] = -rec[a].astype(jnp.float32)
-
     for step in range(n_y):
         part = lax.rem(y + step, n_y)
         if step == 0:
@@ -103,7 +100,7 @@
                 prod = jnp.dot(flat(v[:, a, j]), x[j], preferred_element_type=jnp.float32)
                 coeffs = adjoint_pair(prod, half)
                 for d in range(n_col):
-                    kept = jnp.where(level < ranks[d * tiles + a, j], coeffs[d], 0.0)
+                    kept = jnp.where(level < ranks[j, d * tiles + a], coeffs[d], 0.0)
                     send1[a, d, j] = kept.astype(jnp.bfloat16)
                 return carry
 
@@ -117,6 +114,10 @@
         lax.fori_loop(0, tiles, forward, 0)
 
     u_copy.wait()
+    tile, sources = x.shape[1], x.shape[2] // 2
+    for a in range(tiles):
+        rows = rec[pl.ds(a * tile, tile)].astype(jnp.float32)
+        res[a] = -jnp.concatenate([rows[:, 0], rows[:, 1]], axis=-1)
 
     def middle(a, carry):
         def apply(k, carry):
@@ -149,6 +150,8 @@
         for k in range(1, n_col):
             exchange(send2, recv2, s2, r2, a, lax.rem(col + k, n_col), col, y).start()
         recv2[a, col] = send2[a, col]
+        for c in range(2):
+            res_out[pl.ds(a * tile, tile), c] = res[a, :, c * sources:(c + 1) * sources]
         return carry
 
     lax.fori_loop(0, tiles, middle, 0)
@@ -161,7 +164,7 @@
         def one(t, carry):
             j = part * group + t
             kept = [
-                jnp.where(level < ranks[s * tiles + a, j], recv2[a, s, j].astype(jnp.float32), 0.0).astype(jnp.bfloat16)
+                jnp.where(level < ranks[j, s * tiles + a], recv2[a, s, j].astype(jnp.float32), 0.0).astype(jnp.bfloat16)
                 for s in range(n_col)
             ]
             total[j] += transposed_dot(flat(v[:, a, j]), stacked(jnp.stack(kept)))
@@ -200,10 +203,14 @@
     last(tiles - 1, y)
     core_copy(y).start()
     core_copy(y).wait_recv()
-    grad[...] = total[pl.ds(row * width, width)] + rs1[y]
     for peer in order:
         chip_copy(peer, peer).wait_recv()
-        grad[...] += rs2[peer].astype(jnp.float32)
+    for t in range(width):
+        grad = total[row * width + t] + rs1[y, t]
+        for peer in order:
+            grad += rs2[peer, t].astype(jnp.float32)
+        for c in range(2):
+            grad_out[pl.ds(t * tile, tile), c] = grad[:, c * sources:(c + 1) * sources]
 
     for k in range(1, n_row):
         wave_copy(lax.rem(row + k, n_row), row).wait_send()
@@ -238,12 +245,13 @@
     residual, gradient = pl.pallas_call(
         functools.partial(kernel, n_row, n_col),
         out_shape=(
-            jax.ShapeDtypeStruct((tiles, tile, wide), jnp.float32),
-            jax.ShapeDtypeStruct((width, tile, wide), jnp.float32),
+            jax.ShapeDtypeStruct((tiles * tile, 2, sources), jnp.float32),
+            jax.ShapeDtypeStruct((width * tile, 2, sources), jnp.float32),
         ),
         in_specs=[vmem, vmem, whole, whole, pl.BlockSpec(memory_space=pltpu.SMEM)],
         out_specs=(vmem, vmem),
         scratch_shapes=[
+            pltpu.VMEM((tiles, tile, wide), jnp.float32),
             pltpu.VMEM((n_col, tiles, columns, both, tile), jnp.bfloat16),
             pltpu.VMEM((tiles, n_col, columns, both, tile), jnp.bfloat16),
             pltpu.VMEM((columns, tile, wide), jnp.bfloat16),
@@ -261,12 +269,12 @@
         ),
     )(
         wavefield.reshape(width, tile, wide),
-        recorded.reshape(tiles, tile, wide),
+        recorded,
         v_bases.reshape(n_col, tiles, columns, both, tile),
         u_bases.reshape(tiles, n_col, columns, both, tile),
-        ranks,
+        ranks.T,
     )
-    return residual.reshape(-1, 2, sources), gradient.reshape(-1, 2, sources)
+    return residual, gradient
 
 
 def solution(mesh):

time: 218 us -> 214 us (0.982)
  local copies, waits for them, and re-layouts: 11.1 us -> 6.69 us
    reshape x3 -> x0, local copies, waits for them, and re-layouts: 7.59 us -> none  [the longest x2 5.42 us: body(): return (residual.reshape(-1, 2, sources), gradient.reshape(-1, 2, sources))]
    unnamed x1 -> x2, local copies, waits for them, and re-layouts: 1.37 us -> 4.52 us
where the time goes in v3:
time: 214 us
  Pallas kernels  206 us (96%)
  local copies, waits for them, and re-layouts  6.69 us (3%)
    pallas_call x1, Pallas kernels, body(): pl.pallas_call(functools.partial(kernel, n_row, n_col), out_shape=(jax.Sh...  206 us
    unnamed x2, local copies, waits for them, and re-layouts  4.52 us

profile of v3, /device:TPU:27, one launch (start us, length us, event | category | flops | bytes accessed | tf_op | source)
XLA Modules:
  0.0 213.6 jit_solution(5884080877353078426)
XLA Ops:
  0.6 2.2 %reshape.13.wave = bf16[4,256,256]{2,1,0:T(8,128)(2,1)} reshape(bf16[1024,2,128]{2,1,0:T(2,128)(2,1)} %param.5) | data formatting | bytes 1048576 | tf_op jit(solution)/shard_map/reshape | solution.py:271
  2.8 206.3 %shard_map.68 = (f32[1024,2,128]{2,1,0:T(2,128)}, f32[1024,2,128]{2,1,0:T(2,128)}) custom-call(bf16[4,256,256]{2,1,0:T(8,128)(2,1)} %reshape.13.wave, bf16[1024,2,128]{2,1,0:T(2,128)(2,1)} %rec.1, bf16[8,4,16,32,256]{4,3,2,1,0:T(8,128)(2,1)} %bitcast.3, bf16[4,8,16,32,256]{4,3,2,1,0:T(8,128)(2,1)} %bitcast.4, s32[16,32]{1,0:T(8,128)} %bitcast.5), custom_call_target="tpu_custom_call" | custom-call | tf_op jit(solution)/shard_map/pallas_call | solution.py:245
  209.1 2.3 %copy.9 = f32[1024,2,128]{2,1,0:T(2,128)} copy(f32[1024,2,128]{2,1,0:T(2,128)} %get-tuple-element.4) | data formatting | bytes 2097152
  211.3 2.3 %copy.10 = f32[1024,2,128]{2,1,0:T(2,128)} copy(f32[1024,2,128]{2,1,0:T(2,128)} %get-tuple-element.5) | data formatting | bytes 2097152

commit v4 on v3

--- a/solution.py
+++ b/solution.py
@@ -45,7 +45,8 @@
     n_y = n_row // 2
     tiles, columns = u.shape[0], v.shape[2]
     half = v.shape[3] // 2
-    width = wave.shape[0]
+    tile, sources = x.shape[1], x.shape[2] // 2
+    width = wave.shape[0] // tile
     group = 2 * width
     level = lax.broadcasted_iota(jnp.int32, (half, x.shape[2]), 0)
 
@@ -63,11 +64,14 @@
         pl.semaphore_signal(barrier, inc=1, device_id={"col": lax.rem(col + k, n_col)}, device_id_type=MESH)
     for k in range(1, n_row):
         pl.semaphore_signal(barrier, inc=1, device_id={"row": lax.rem(row + k, n_row)}, device_id_type=MESH)
+    for t in range(width):
+        rows = wave[pl.ds(t * tile, tile)].astype(jnp.float32)
+        x[row * width + t] = jnp.concatenate([rows[:, 0], rows[:, 1]], axis=-1).astype(jnp.bfloat16)
     pl.semaphore_wait(barrier, n_col + n_row - 2)
 
     def wave_copy(peer, origin):
         return pltpu.make_async_remote_copy(
-            src_ref=wave, dst_ref=x.at[pl.ds(origin * width, width)],
+            src_ref=x.at[pl.ds(row * width, width)], dst_ref=x.at[pl.ds(origin * width, width)],
             send_sem=xs.at[peer], recv_sem=xr.at[origin],
             device_id={"row": peer}, device_id_type=MESH)
 
@@ -82,7 +86,6 @@
     for k in range(1, n_y):
         for c in range(2):
             wave_copy(2 * lax.rem(y + k, n_y) + c, row).start()
-    x[pl.ds(row * width, width)] = wave[...]
     total[...] = jnp.zeros_like(total)
     for step in range(n_y):
         part = lax.rem(y + step, n_y)
@@ -114,7 +117,6 @@
         lax.fori_loop(0, tiles, forward, 0)
 
     u_copy.wait()
-    tile, sources = x.shape[1], x.shape[2] // 2
     for a in range(tiles):
         rows = rec[pl.ds(a * tile, tile)].astype(jnp.float32)
         res[a] = -jnp.concatenate([rows[:, 0], rows[:, 1]], axis=-1)
@@ -268,7 +270,7 @@
             collective_id=0, has_side_effects=True, vmem_limit_bytes=58 * 2**20
         ),
     )(
-        wavefield.reshape(width, tile, wide),
+        wavefield,
         recorded,
         v_bases.reshape(n_col, tiles, columns, both, tile),
         u_bases.reshape(tiles, n_col, columns, both, tile),

time: 214 us -> 212 us (level)
  local copies, waits for them, and re-layouts: 6.69 us -> 4.52 us
    reshape x1 -> x0, local copies, waits for them, and re-layouts: 2.17 us -> none  [body(): wavefield.reshape(width, tile, wide)]
where the time goes in v4:
time: 212 us; the launch traced here: 211 us
  Pallas kernels  206 us (97%)
  local copies, waits for them, and re-layouts  4.52 us (2%)
    pallas_call x1, Pallas kernels, body(): pl.pallas_call(functools.partial(kernel, n_row, n_col), out_shape=(jax.Sh...  206 us
    unnamed x2, local copies, waits for them, and re-layouts  4.52 us

profile of v4, /device:TPU:27, one launch (start us, length us, event | category | flops | bytes accessed | tf_op | source)
XLA Modules:
  0.0 211.5 jit_solution(17926171906401181396)
XLA Ops:
  0.6 206.3 %shard_map.68 = (f32[1024,2,128]{2,1,0:T(2,128)}, f32[1024,2,128]{2,1,0:T(2,128)}) custom-call(bf16[1024,2,128]{2,1,0:T(2,128)(2,1)} %wave.1, bf16[1024,2,128]{2,1,0:T(2,128)(2,1)} %rec.1, bf16[8,4,16,32,256]{4,3,2,1,0:T(8,128)(2,1)} %bitcast.3, bf16[4,8,16,32,256]{4,3,2,1,0:T(8,128)(2,1)} %bitcast.4, s32[16,32]{1,0:T(8,128)} %bitcast.5), custom_call_target="tpu_custom_call" | custom-call | tf_op jit(solution)/shard_map/pallas_call | solution.py:247
  206.9 2.3 %copy.9 = f32[1024,2,128]{2,1,0:T(2,128)} copy(f32[1024,2,128]{2,1,0:T(2,128)} %get-tuple-element.4) | data formatting | bytes 2097152
  209.2 2.3 %copy.10 = f32[1024,2,128]{2,1,0:T(2,128)} copy(f32[1024,2,128]{2,1,0:T(2,128)} %get-tuple-element.5) | data formatting | bytes 2097152
